TPU v7x, 128 devices: a whole 4x4x4 slice. The times are simulated.
128 devices in a mesh: inst: 16 (over z_hi, y, core), blk: 8 (over x, z_lo).
Axes of the slice: x: 4, y: 4, z: 4 (z_hi: 2, z_lo: 2; z = z_hi * 2 + z_lo), core: 2. Of those that a mesh axis runs over, the one named last changes fastest.
Arguments:
- queries: bfloat16 [16384, 8192], P(('inst', 'blk')), may hold values from -16 to 16
- keys: bfloat16 [16384, 1024], P(('inst', 'blk')), may hold values from -16 to 16
- values: bfloat16 [16384, 1024], P(('inst', 'blk')), may hold values from -6 to 6
- lengths: int32 [8], replicated, may hold values from 1 to 4, as said below
Outputs:
- attended: bfloat16 [16384, 8192], P(('inst', 'blk'))
Inputs may be any that keep to these rules, and one draw needn't show every extreme that they name: The lengths sum to 16; one request covers exactly 4 instances.
All inputs are finite; a program needn't handle non-finite values.
Results may differ from a plain program's by a relative error of at most 0.0085.
Values may be sent and summed in bfloat16 or wider, within the bound.
A program may use at most 320 MiB of HBM per device.

v0:
```python
import math

import jax
import jax.numpy as jnp
from jax import lax
from jax.sharding import PartitionSpec as P

QUERY_HEADS = 64
KEY_VALUE_HEADS = 8
HEAD_SIZE = 128
MAXSPAN = 4


def passed_along(value, axis, by):
    devices = lax.axis_size(axis)
    pairs = [(i, i + by) for i in range(devices) if 0 <= i + by < devices]
    return lax.ppermute(value, axis, pairs)


def absorb(state, token_slab, kpos, query_heads, qpos, lowest):
    count_keys = token_slab.shape[1]
    block_slice = math.gcd(count_keys, 256)
    item_count = count_keys // block_slice
    key_tiles = token_slab[0].reshape(item_count, block_slice, KEY_VALUE_HEADS, HEAD_SIZE)
    value_tiles = token_slab[1].reshape(item_count, block_slice, KEY_VALUE_HEADS, HEAD_SIZE)
    pos_blocks = kpos.reshape(item_count, block_slice)
    scale = HEAD_SIZE ** (-0.5)

    def step(carry, item):
        best_option, grand_total, summed_output = carry
        key_block, value_block, pos_block = item
        mask = (pos_block[None, :] >= lowest) & (pos_block[None, :] <= qpos[:, None])
        wide_mask = mask[:, None, None, :]
        scores = (
            jnp.einsum("chgd,khd->chgk", query_heads, key_block, preferred_element_type=jnp.float32)
            * scale
        )
        scores = jnp.where(wide_mask, scores, -1e30)
        new_best = jnp.maximum(best_option, jnp.max(scores, axis=-1))
        weights = jnp.where(wide_mask, jnp.exp(scores - new_best[..., None]), 0.0)
        factor = jnp.exp(best_option - new_best)
        grand_total = grand_total * factor + jnp.sum(weights, axis=-1)
        update = jnp.einsum(
            "chgk,khd->chgd",
            weights.astype(jnp.bfloat16),
            value_block,
            preferred_element_type=jnp.float32,
        )
        summed_output = summed_output * factor[..., None] + update
        return ((new_best, grand_total, summed_output), None)

    return lax.scan(step, state, (key_tiles, value_tiles, pos_blocks))[0]


def local(queries, keys, values, lengths):
    token_count = queries.shape[0]
    width = lax.axis_size("blk")
    stretch_factor = width * token_count
    here = lax.axis_index("inst")
    spot = lax.axis_index("blk")
    ends = jnp.cumsum(lengths)
    start_inst = jnp.max(jnp.where(ends <= here, ends, 0))
    lowest = start_inst * stretch_factor
    qpos = here * stretch_factor + spot * token_count + jnp.arange(token_count, dtype=jnp.int32)
    query_heads = queries.reshape(
        token_count, KEY_VALUE_HEADS, QUERY_HEADS // KEY_VALUE_HEADS, HEAD_SIZE
    )
    best_option = jnp.full(
        (token_count, KEY_VALUE_HEADS, QUERY_HEADS // KEY_VALUE_HEADS), -1e30, jnp.float32
    )
    grand_total = jnp.zeros(
        (token_count, KEY_VALUE_HEADS, QUERY_HEADS // KEY_VALUE_HEADS), jnp.float32
    )
    summed_output = jnp.zeros(
        (token_count, KEY_VALUE_HEADS, QUERY_HEADS // KEY_VALUE_HEADS, HEAD_SIZE), jnp.float32
    )
    state = (best_option, grand_total, summed_output)
    stacked = jnp.stack([keys, values])
    whole = lax.all_gather(stacked, "blk", axis=1, tiled=True)
    own_pos = here * stretch_factor + jnp.arange(stretch_factor, dtype=jnp.int32)
    state = absorb(state, whole, own_pos, query_heads, qpos, lowest)
    for dist in range(1, MAXSPAN):
        remote = passed_along(whole, "inst", dist)
        remote_pos = (here - dist) * stretch_factor + jnp.arange(stretch_factor, dtype=jnp.int32)
        state = absorb(state, remote, remote_pos, query_heads, qpos, lowest)
    best_option, grand_total, summed_output = state
    attended = summed_output / grand_total[..., None]
    return attended.reshape(token_count, QUERY_HEADS * HEAD_SIZE).astype(jnp.bfloat16)


def solution(mesh):
    in_specs = (P(("inst", "blk"), None), P(("inst", "blk"), None), P(("inst", "blk"), None), P())
    out_specs = P(("inst", "blk"), None)
    return jax.shard_map(local, mesh=mesh, in_specs=in_specs, out_specs=out_specs, check_vma=False)
```

profile of v0, /device:TPU:65, one launch (start us, length us, event | category | flops | bytes accessed | tf_op | source)
XLA Modules:
  0.0 459.8 jit_solution(7175633624234760815)
XLA Ops:
  10.6 4.1 copy.14
  18.4 81.7 %all-gather.2.cloned.1.call-done = bf16[2,1024,1024]{2,1,0:T(8,128)(2,1)} async-done(((bf16[2,128,1024]{2,1,0:T(8,128)(2,1)}), bf16[2,1024,1024]{2,1,0:T(8,128)(2,1)}) %all-gather.2.cloned.1.call-update) | async-done | bytes 4194320 | tf_op jit(solution)/shard_map/all_gather | solution.py:79
  111.0 78.2 %while.63 = (s32[]{:T(128)}, f32[128,8,8]{0,2,1:T(8,128)S(1)}, f32[128,8,8]{0,2,1:T(8,128)S(1)}, f32[128,8,8,128]{0,3,2,1:T(8,128)}, s32[4,256]{1,0:T(4,128)S(1)...) while((s32[]{:T(128)}, f32[128,8,8]{0,2,1:T(8,128)S(1)}, ...), condition=%wide.region_5.6_spmd.clone, body=%wide.region_2.5_spmd.clone.sunk | while | flops 1104257408 | bytes 40506000 | solution.py:52
  112.5 4.6 fusion.125
  117.1 4.5 fusion.126
  121.9 7.8 %bitcast_add_fusion.11 = f32[128,8,8,128]{0,3,2,1:T(8,128)} fusion(f32[128,8,8,128]{0,3,2,1:T(8,128)} %get-tuple-element.819, f32[128,8,8]{0,2,1:T(8,128)S(1)} %get-tuple-element.802, pred[]{:T(512)S(6)} %compare.3, f32[8,256,128,8]{2,1,3,0:T(8,128)} %get-tuple-element.800, f32[128,8,8]{0,2,1:T(8,128)S(1)} %select_maximum_fusion.2, ...), kind=kOutput, calls=%fused_computation.88.clone.1 | convolution fusion | flops 550502400 | bytes 17399808 | tf_op jit(solution)/shard_map/while/body/eval_jaxpr/chgk,khd->chgd/dot_general | solution.py:43
  131.1 4.6 fusion.125
  135.7 4.5 fusion.126
  140.6 9.0 %bitcast_add_fusion.11 = f32[128,8,8,128]{0,3,2,1:T(8,128)} fusion(f32[128,8,8,128]{0,3,2,1:T(8,128)} %get-tuple-element.819, f32[128,8,8]{0,2,1:T(8,128)S(1)} %get-tuple-element.802, pred[]{:T(512)S(6)} %compare.3, f32[8,256,128,8]{2,1,3,0:T(8,128)} %get-tuple-element.800, f32[128,8,8]{0,2,1:T(8,128)S(1)} %select_maximum_fusion.2, ...), kind=kOutput, calls=%fused_computation.88.clone.1 | convolution fusion | flops 550502400 | bytes 17399808 | tf_op jit(solution)/shard_map/while/body/eval_jaxpr/chgk,khd->chgd/dot_general | solution.py:43
  151.0 4.6 fusion.125
  155.5 4.5 fusion.126
  160.4 9.0 %bitcast_add_fusion.11 = f32[128,8,8,128]{0,3,2,1:T(8,128)} fusion(f32[128,8,8,128]{0,3,2,1:T(8,128)} %get-tuple-element.819, f32[128,8,8]{0,2,1:T(8,128)S(1)} %get-tuple-element.802, pred[]{:T(512)S(6)} %compare.3, f32[8,256,128,8]{2,1,3,0:T(8,128)} %get-tuple-element.800, f32[128,8,8]{0,2,1:T(8,128)S(1)} %select_maximum_fusion.2, ...), kind=kOutput, calls=%fused_computation.88.clone.1 | convolution fusion | flops 550502400 | bytes 17399808 | tf_op jit(solution)/shard_map/while/body/eval_jaxpr/chgk,khd->chgd/dot_general | solution.py:43
  170.8 4.6 fusion.125
  175.4 4.5 fusion.126
  180.2 9.0 %bitcast_add_fusion.11 = f32[128,8,8,128]{0,3,2,1:T(8,128)} fusion(f32[128,8,8,128]{0,3,2,1:T(8,128)} %get-tuple-element.819, f32[128,8,8]{0,2,1:T(8,128)S(1)} %get-tuple-element.802, pred[]{:T(512)S(6)} %compare.3, f32[8,256,128,8]{2,1,3,0:T(8,128)} %get-tuple-element.800, f32[128,8,8]{0,2,1:T(8,128)S(1)} %select_maximum_fusion.2, ...), kind=kOutput, calls=%fused_computation.88.clone.1 | convolution fusion | flops 550502400 | bytes 17399808 | tf_op jit(solution)/shard_map/while/body/eval_jaxpr/chgk,khd->chgd/dot_general | solution.py:43
  202.8 60.9 %while.60 = (s32[]{:T(128)}, f32[128,8,8]{0,2,1:T(8,128)S(1)}, f32[128,8,8]{0,2,1:T(8,128)S(1)}, f32[128,8,8,128]{0,3,2,1:T(8,128)}, s32[4,256]{1,0:T(4,128)S(1)...) while((s32[]{:T(128)}, f32[128,8,8]{0,2,1:T(8,128)S(1)}, ...), condition=%wide.region_9.10_spmd.clone, body=%wide.region_6.9_spmd.clone.sunk | while | flops 1103184256 | bytes 74060440 | solution.py:52
  209.2 8.8 %bitcast_add_fusion.8 = f32[128,8,8,128]{0,3,2,1:T(8,128)} fusion(f32[128,8,8,128]{0,3,2,1:T(8,128)} %get-tuple-element.854, f32[128,8,8]{0,2,1:T(8,128)S(1)} %get-tuple-element.748, f32[8,256,128,8]{2,1,3,0:T(8,128)} %copy-done, f32[128,8,8]{0,2,1:T(8,128)S(1)} %max.21, pred[128,256]{0,1:T(8,128)(4,1)S(1)} %compare_and_fusion.8, ...), kind=kOutput, calls=%fused_computation.10.clone.1 | convolution fusion | flops 549453824 | bytes 17399808 | tf_op jit(solution)/shard_map/while/body/eval_jaxpr/chgk,khd->chgd/dot_general | solution.py:43
  224.4 8.8 %bitcast_add_fusion.8 = f32[128,8,8,128]{0,3,2,1:T(8,128)} fusion(f32[128,8,8,128]{0,3,2,1:T(8,128)} %get-tuple-element.854, f32[128,8,8]{0,2,1:T(8,128)S(1)} %get-tuple-element.748, f32[8,256,128,8]{2,1,3,0:T(8,128)} %copy-done, f32[128,8,8]{0,2,1:T(8,128)S(1)} %max.21, pred[128,256]{0,1:T(8,128)(4,1)S(1)} %compare_and_fusion.8, ...), kind=kOutput, calls=%fused_computation.10.clone.1 | convolution fusion | flops 549453824 | bytes 17399808 | tf_op jit(solution)/shard_map/while/body/eval_jaxpr/chgk,khd->chgd/dot_general | solution.py:43
  239.6 8.8 %bitcast_add_fusion.8 = f32[128,8,8,128]{0,3,2,1:T(8,128)} fusion(f32[128,8,8,128]{0,3,2,1:T(8,128)} %get-tuple-element.854, f32[128,8,8]{0,2,1:T(8,128)S(1)} %get-tuple-element.748, f32[8,256,128,8]{2,1,3,0:T(8,128)} %copy-done, f32[128,8,8]{0,2,1:T(8,128)S(1)} %max.21, pred[128,256]{0,1:T(8,128)(4,1)S(1)} %compare_and_fusion.8, ...), kind=kOutput, calls=%fused_computation.10.clone.1 | convolution fusion | flops 549453824 | bytes 17399808 | tf_op jit(solution)/shard_map/while/body/eval_jaxpr/chgk,khd->chgd/dot_general | solution.py:43
  254.9 8.8 %bitcast_add_fusion.8 = f32[128,8,8,128]{0,3,2,1:T(8,128)} fusion(f32[128,8,8,128]{0,3,2,1:T(8,128)} %get-tuple-element.854, f32[128,8,8]{0,2,1:T(8,128)S(1)} %get-tuple-element.748, f32[8,256,128,8]{2,1,3,0:T(8,128)} %copy-done, f32[128,8,8]{0,2,1:T(8,128)S(1)} %max.21, pred[128,256]{0,1:T(8,128)(4,1)S(1)} %compare_and_fusion.8, ...), kind=kOutput, calls=%fused_computation.10.clone.1 | convolution fusion | flops 549453824 | bytes 17399808 | tf_op jit(solution)/shard_map/while/body/eval_jaxpr/chgk,khd->chgd/dot_general | solution.py:43
  263.7 23.5 %collective-permute-done.1 = bf16[2,1024,1024]{2,1,0:T(8,128)(2,1)} collective-permute-done((bf16[2,1024,1024]{2,1,0:T(8,128)(2,1)}, bf16[2,1024,1024]{2,1,0:T(8,128)(2,1)}, u32[]{:S(2)}, u32[]{:S(2)}) %collective-permute-start.1) | collective-permute-done | bytes 4194336 | tf_op jit(solution)/shard_map/ppermute | solution.py:17
  294.4 60.9 %while.61 = (s32[]{:T(128)}, f32[128,8,8]{0,2,1:T(8,128)S(1)}, f32[128,8,8]{0,2,1:T(8,128)S(1)}, f32[128,8,8,128]{0,3,2,1:T(8,128)}, s32[4,256]{1,0:T(4,128)S(1)...) while((s32[]{:T(128)}, f32[128,8,8]{0,2,1:T(8,128)S(1)}, ...), condition=%wide.region_13.14_spmd.clone, body=%wide.region_10.13_spmd.clone.sunk | while | flops 1103184256 | bytes 74060440 | solution.py:52
  300.7 8.8 %bitcast_add_fusion.9 = f32[128,8,8,128]{0,3,2,1:T(8,128)} fusion(f32[128,8,8,128]{0,3,2,1:T(8,128)} %get-tuple-element.887, f32[128,8,8]{0,2,1:T(8,128)S(1)} %get-tuple-element.766, f32[8,256,128,8]{2,1,3,0:T(8,128)} %copy-done.1, f32[128,8,8]{0,2,1:T(8,128)S(1)} %max.22, pred[128,256]{0,1:T(8,128)(4,1)S(1)} %compare_and_fusion.9, ...), kind=kOutput, calls=%fused_computation.36.clone.1 | convolution fusion | flops 549453824 | bytes 17399808 | tf_op jit(solution)/shard_map/while/body/eval_jaxpr/chgk,khd->chgd/dot_general | solution.py:43
  315.9 8.8 %bitcast_add_fusion.9 = f32[128,8,8,128]{0,3,2,1:T(8,128)} fusion(f32[128,8,8,128]{0,3,2,1:T(8,128)} %get-tuple-element.887, f32[128,8,8]{0,2,1:T(8,128)S(1)} %get-tuple-element.766, f32[8,256,128,8]{2,1,3,0:T(8,128)} %copy-done.1, f32[128,8,8]{0,2,1:T(8,128)S(1)} %max.22, pred[128,256]{0,1:T(8,128)(4,1)S(1)} %compare_and_fusion.9, ...), kind=kOutput, calls=%fused_computation.36.clone.1 | convolution fusion | flops 549453824 | bytes 17399808 | tf_op jit(solution)/shard_map/while/body/eval_jaxpr/chgk,khd->chgd/dot_general | solution.py:43
  331.2 8.8 %bitcast_add_fusion.9 = f32[128,8,8,128]{0,3,2,1:T(8,128)} fusion(f32[128,8,8,128]{0,3,2,1:T(8,128)} %get-tuple-element.887, f32[128,8,8]{0,2,1:T(8,128)S(1)} %get-tuple-element.766, f32[8,256,128,8]{2,1,3,0:T(8,128)} %copy-done.1, f32[128,8,8]{0,2,1:T(8,128)S(1)} %max.22, pred[128,256]{0,1:T(8,128)(4,1)S(1)} %compare_and_fusion.9, ...), kind=kOutput, calls=%fused_computation.36.clone.1 | convolution fusion | flops 549453824 | bytes 17399808 | tf_op jit(solution)/shard_map/while/body/eval_jaxpr/chgk,khd->chgd/dot_general | solution.py:43
  346.4 8.8 %bitcast_add_fusion.9 = f32[128,8,8,128]{0,3,2,1:T(8,128)} fusion(f32[128,8,8,128]{0,3,2,1:T(8,128)} %get-tuple-element.887, f32[128,8,8]{0,2,1:T(8,128)S(1)} %get-tuple-element.766, f32[8,256,128,8]{2,1,3,0:T(8,128)} %copy-done.1, f32[128,8,8]{0,2,1:T(8,128)S(1)} %max.22, pred[128,256]{0,1:T(8,128)(4,1)S(1)} %compare_and_fusion.9, ...), kind=kOutput, calls=%fused_computation.36.clone.1 | convolution fusion | flops 549453824 | bytes 17399808 | tf_op jit(solution)/shard_map/while/body/eval_jaxpr/chgk,khd->chgd/dot_general | solution.py:43
  355.2 21.3 %collective-permute-done.2 = bf16[2,1024,1024]{2,1,0:T(8,128)(2,1)} collective-permute-done((bf16[2,1024,1024]{2,1,0:T(8,128)(2,1)}, bf16[2,1024,1024]{2,1,0:T(8,128)(2,1)}, u32[]{:S(2)}, u32[]{:S(2)}) %collective-permute-start.2) | collective-permute-done | bytes 4194336 | tf_op jit(solution)/shard_map/ppermute | solution.py:17
  383.7 63.6 %while.62 = (s32[]{:T(128)}, f32[128,8,8]{0,2,1:T(8,128)S(1)}, f32[128,8,8]{0,2,1:T(8,128)S(1)}, f32[128,8,8,128]{0,3,2,1:T(8,128)}, s32[4,256]{1,0:T(4,128)}, /...) while((s32[]{:T(128)}, f32[128,8,8]{0,2,1:T(8,128)S(1)}, ...), condition=%wide.region_17.18_spmd.clone, body=%wide.region_14.17_spmd.clone.sunk | while | flops 1103184256 | bytes 74060440 | solution.py:52
  390.8 8.8 %bitcast_add_fusion.10 = f32[128,8,8,128]{0,3,2,1:T(8,128)} fusion(f32[128,8,8,128]{0,3,2,1:T(8,128)} %get-tuple-element.920, f32[128,8,8]{0,2,1:T(8,128)S(1)} %get-tuple-element.784, f32[8,256,128,8]{2,1,3,0:T(8,128)} %copy-done.2, f32[128,8,8]{0,2,1:T(8,128)S(1)} %max.23, pred[128,256]{0,1:T(8,128)(4,1)S(1)} %compare_and_fusion.10, ...), kind=kOutput, calls=%fused_computation.62.clone.1 | convolution fusion | flops 549453824 | bytes 17399808 | tf_op jit(solution)/shard_map/while/body/eval_jaxpr/chgk,khd->chgd/dot_general | solution.py:43
  406.7 8.8 %bitcast_add_fusion.10 = f32[128,8,8,128]{0,3,2,1:T(8,128)} fusion(f32[128,8,8,128]{0,3,2,1:T(8,128)} %get-tuple-element.920, f32[128,8,8]{0,2,1:T(8,128)S(1)} %get-tuple-element.784, f32[8,256,128,8]{2,1,3,0:T(8,128)} %copy-done.2, f32[128,8,8]{0,2,1:T(8,128)S(1)} %max.23, pred[128,256]{0,1:T(8,128)(4,1)S(1)} %compare_and_fusion.10, ...), kind=kOutput, calls=%fused_computation.62.clone.1 | convolution fusion | flops 549453824 | bytes 17399808 | tf_op jit(solution)/shard_map/while/body/eval_jaxpr/chgk,khd->chgd/dot_general | solution.py:43
  422.6 8.8 %bitcast_add_fusion.10 = f32[128,8,8,128]{0,3,2,1:T(8,128)} fusion(f32[128,8,8,128]{0,3,2,1:T(8,128)} %get-tuple-element.920, f32[128,8,8]{0,2,1:T(8,128)S(1)} %get-tuple-element.784, f32[8,256,128,8]{2,1,3,0:T(8,128)} %copy-done.2, f32[128,8,8]{0,2,1:T(8,128)S(1)} %max.23, pred[128,256]{0,1:T(8,128)(4,1)S(1)} %compare_and_fusion.10, ...), kind=kOutput, calls=%fused_computation.62.clone.1 | convolution fusion | flops 549453824 | bytes 17399808 | tf_op jit(solution)/shard_map/while/body/eval_jaxpr/chgk,khd->chgd/dot_general | solution.py:43
  438.4 8.8 %bitcast_add_fusion.10 = f32[128,8,8,128]{0,3,2,1:T(8,128)} fusion(f32[128,8,8,128]{0,3,2,1:T(8,128)} %get-tuple-element.920, f32[128,8,8]{0,2,1:T(8,128)S(1)} %get-tuple-element.784, f32[8,256,128,8]{2,1,3,0:T(8,128)} %copy-done.2, f32[128,8,8]{0,2,1:T(8,128)S(1)} %max.23, pred[128,256]{0,1:T(8,128)(4,1)S(1)} %compare_and_fusion.10, ...), kind=kOutput, calls=%fused_computation.62.clone.1 | convolution fusion | flops 549453824 | bytes 17399808 | tf_op jit(solution)/shard_map/while/body/eval_jaxpr/chgk,khd->chgd/dot_general | solution.py:43
  (207 shorter events, 137.3 us)
Async XLA Ops:
  6.5 93.5 %all-gather.2.cloned.1.call-start = ((), (), s32[]{:S(2)}) async-start(), calls=%async_computation | async-start | bytes 4718592 | tf_op jit(solution)/shard_map/all_gather | solution.py:79
  107.2 88.5 %collective-permute-start = (bf16[2,1024,1024]{2,1,0:T(8,128)(2,1)}, bf16[2,1024,1024]{2,1,0:T(8,128)(2,1)}, u32[]{:S(2)}, u32[]{:S(2)}) collective-permute-start(bf16[2,1024,1024]{2,1,0:T(8,128)(2,1)} %all-gather.2.cloned.1.call-done), channel_id=1, source_target_pairs={{0,8},{8,16},{16,24},{24,32},{32,40},{40,48},{48,56},{56,64},{64,7... | collective-permute-start | bytes 12582920 | tf_op jit(solution)/shard_map/ppermute | solution.py:17
  189.2 98.1 %collective-permute-start.1 = (bf16[2,1024,1024]{2,1,0:T(8,128)(2,1)}, bf16[2,1024,1024]{2,1,0:T(8,128)(2,1)}, u32[]{:S(2)}, u32[]{:S(2)}) collective-permute-start(bf16[2,1024,1024]{2,1,0:T(8,128)(2,1)} %all-gather.2.cloned.1.call-done), channel_id=1, source_target_pairs={{0,16},{8,24},{16,32},{24,40},{32,48},{40,56},{48,64},{56,72},{64,... | collective-permute-start | bytes 12582920 | tf_op jit(solution)/shard_map/ppermute | solution.py:17
  192.3 184.3 %collective-permute-start.2 = (bf16[2,1024,1024]{2,1,0:T(8,128)(2,1)}, bf16[2,1024,1024]{2,1,0:T(8,128)(2,1)}, u32[]{:S(2)}, u32[]{:S(2)}) collective-permute-start(bf16[2,1024,1024]{2,1,0:T(8,128)(2,1)} %all-gather.2.cloned.1.call-done), channel_id=1, source_target_pairs={{0,24},{8,32},{16,40},{24,48},{32,56},{40,64},{48,72},{56,80},{64,... | collective-permute-start | bytes 12582920 | tf_op jit(solution)/shard_map/ppermute | solution.py:17
  205.6 3.2 copy-start
  220.9 3.2 copy-start
  236.1 3.2 copy-start
  251.3 3.2 copy-start
  297.2 3.2 copy-start.1
  312.4 3.2 copy-start.1
  327.6 3.2 copy-start.1
  342.8 3.2 copy-start.1
  387.2 3.2 copy-start.2
  403.1 3.2 copy-start.2
  419.0 3.2 copy-start.2
  434.9 3.2 copy-start.2
Sparse Core Ops, SparseCore 0:
  9.0 91.0 all-gather.1
where the time goes:
time: 462 us; the launch traced here: 460 us
  matrix products  175 us (38%)
  waiting for transfers between devices  127 us (27%)
  local copies, waits for them, and re-layouts  77.6 us (17%)
  other arithmetic  55.3 us (12%)
  between operations  14.2 us (3%)
  starting transfers between devices  10.4 us (2%)
    dot_general x16, matrix products, step(): jnp.einsum('chgk,khd->chgd', weights.astype(jnp.bfloat16), value_block, p...  141 us
    all_gather x1, waiting for transfers between devices, local(): whole = lax.all_gather(stacked, 'blk', axis=1, tiled=True)  81.7 us
    ppermute x3, waiting for transfers between devices, passed_along(): return lax.ppermute(value, axis, pairs)  44.9 us
    reduce_sum x16, other arithmetic, step(): grand_total = grand_total * factor + jnp.sum(weights, axis=-1)  42.9 us
    unnamed x14, local copies, waits for them, and re-layouts  35.6 us
    dot_general x16, matrix products, step(): jnp.einsum('chgd,khd->chgk', query_heads, key_block, preferred_element_ty...  34.3 us
    dynamic_slice x32, local copies, waits for them, and re-layouts, absorb(): return lax.scan(step, state, (key_tiles, value_tiles, pos_blocks))[0]  25.6 us
    while x40, local copies, waits for them, and re-layouts  13.5 us
  transfers between devices with their start and end apart: 4, of which 3 were waited for; matrix products, arithmetic and copies ran while one was open for 46% of the time, Pallas kernels for 0%

commit v1 on v0

v1 whole, which is shorter than its diff:
```python
import itertools
import math

import jax
import jax.numpy as jnp
from jax import lax
from jax.experimental import pallas as pl
from jax.experimental.pallas import tpu as pltpu
from jax.sharding import PartitionSpec as P

MESH = pl.DeviceIdType.MESH
HEAD = 128
TOK = 128
GROUPS = 4
HB = 4
ROWS = HB * TOK
HALF = GROUPS * HEAD
SCALE = HEAD**-0.5 * math.log2(math.e)
FAR = 1e30

JOBS = (
    ((0, True, "x"), (1, True, "x"),),
    ((0, True, "xl"), (1, True, "xl"), (0, True, "xr"), (1, True, "xr"), (0, False, "x"), (1, False, "x"),),
    ((2, True, "x"), (3, True, "x"), (2, False, "x"), (3, False, "x"),),
    ((0, False, "xl"), (0, False, "xr"), (0, True, "xx"), (0, False, "xx"), (1, False, "xl"), (1, False, "xr"), (1, True, "xx"), (1, False, "xx"),),
    ((2, True, "xl"), (2, True, "xr"), (3, True, "xl"), (3, True, "xr"),),
    ((4, True, "x"), (4, False, "x"), (4, True, "xl"), (4, True, "xr"),),
    ((2, False, "xl"), (2, False, "xr"), (3, False, "xl"), (3, False, "xr"),),
    ((4, True, "xx"), (4, False, "xx"), (4, False, "xl"), (4, False, "xr"),),
    ((2, True, "xx"), (2, False, "xx"), (3, True, "xx"), (3, False, "xx"),),
)
EVENTS = (
    (1, 0, False, "x", 0),
    (2, 0, False, "x", 1),
    (3, 2, True, "x", 0),
    (4, 1, True, "xl", 0),
    (4, 0, True, "xr", 0),
    (4, 1, True, "xr", 0),
    (4, 1, False, "x", 0),
    (4, 0, True, "xl", 0),
    (5, 0, True, "xl", 1),
    (5, 2, True, "x", 1),
    (6, 3, True, "x", 0),
    (6, 1, True, "xl", 1),
    (6, 1, True, "xr", 1),
    (6, 0, True, "xr", 1),
    (6, 1, False, "x", 1),
    (7, 3, True, "x", 1),
    (7, 0, False, "xl", 1),
    (7, 0, False, "xr", 1),
    (7, 0, False, "xr", 0),
    (7, 0, False, "xl", 0),
    (7, 2, False, "x", 0),
    (8, 2, False, "x", 1),
    (8, 3, True, "xl", 0),
    (8, 1, False, "xl", 0),
    (8, 1, True, "xx", 0),
    (8, 3, False, "x", 0),
    (9, 2, True, "xr", 0),
    (10, 1, False, "xr", 0),
    (10, 3, False, "x", 1),
    (10, 0, True, "xx", 0),
    (11, 1, True, "xx", 1),
    (11, 0, True, "xx", 1),
    (11, 1, False, "xx", 0),
    (12, 3, True, "xr", 0),
    (12, 2, True, "xl", 0),
    (12, 1, False, "xr", 1),
    (12, 0, False, "xx", 0),
    (13, 1, False, "xl", 1),
    (14, 2, False, "xl", 0),
    (14, 4, True, "x", 0),
    (14, 1, False, "xx", 1),
    (14, 2, True, "xl", 1),
    (14, 0, False, "xx", 1),
    (16, 3, True, "xl", 1),
    (16, 4, False, "x", 0),
    (18, 2, True, "xr", 1),
    (18, 2, False, "xr", 0),
    (18, 3, True, "xr", 1),
    (19, 4, True, "x", 1),
    (20, 4, True, "xl", 0),
    (20, 4, True, "xr", 0),
    (21, 3, True, "xx", 0),
    (22, 3, False, "xr", 1),
    (22, 3, False, "xr", 0),
    (22, 4, True, "xl", 1),
    (22, 4, True, "xr", 1),
    (22, 3, False, "xl", 0),
    (22, 4, False, "x", 1),
    (22, 3, False, "xl", 1),
    (23, 2, False, "xl", 1),
    (23, 2, True, "xx", 0),
    (24, 4, False, "xr", 0),
    (24, 4, True, "xx", 0),
    (25, 4, False, "xr", 1),
    (26, 4, True, "xx", 1),
    (26, 2, False, "xr", 1),
    (27, 4, False, "xl", 1),
    (28, 4, False, "xx", 0),
    (28, 3, True, "xx", 1),
    (28, 2, True, "xx", 1),
    (28, 4, False, "xl", 0),
    (30, 4, False, "xx", 1),
    (31, 3, False, "xx", 0),
    (32, 2, False, "xx", 0),
    (32, 3, False, "xx", 1),
    (34, 2, False, "xx", 1),
)
RELAY = (
    (0, 2, "x", 0),
    (3, 2, "x", 1),
    (4, 3, "x", 0),
    (5, 3, "x", 1),
    (6, 3, "xl", 0),
    (6, 2, "xr", 0),
    (7, 3, "xr", 0),
    (8, 2, "xl", 0),
    (9, 2, "xl", 1),
    (10, 4, "x", 0),
    (12, 3, "xl", 1),
    (12, 3, "xr", 1),
    (13, 2, "xr", 1),
    (14, 4, "x", 1),
    (14, 3, "xx", 0),
    (15, 2, "xx", 0),
    (15, 3, "xx", 1),
    (15, 2, "xx", 1),
)


def kernel(len_ref, q_ref, k_ref, v_ref, o_ref, kv, stage_s, kin, vin, qbuf, obuf, acc_s, m_s, l_s, bias_s,
           rs, ss, loc, core_send, core_recv, osem):
    inst, b = lax.axis_index("inst"), lax.axis_index("blk")
    c, row = lax.rem(inst, 2), inst // 2
    other = 1 - c
    z, x = lax.rem(b, 2), b // 2
    zo = 1 - z
    xr, xl, xx = lax.rem(x + 1, 4), lax.rem(x + 3, 4), lax.rem(x + 2, 4)
    dev_xr, dev_xl = (inst, xr * 2 + z), (inst, xl * 2 + z)
    dev_z = (inst, x * 2 + zo)
    dev_core = (inst + 1 - 2 * c, b)
    y, zh = lax.rem(row, 4), row // 4
    dev_up = ((zh * 4 + lax.rem(y + 1, 4)) * 2 + c, b)
    dev_down = ((zh * 4 + lax.rem(y + 3, 4)) * 2 + c, b)
    dev_outer = ((4 - row) * 2 + c, x * 2 + zo)
    at_end = jnp.logical_or(row == 0, row == 4)
    z1 = jnp.where(row == 4, zo, z)
    z2 = jnp.where(jnp.logical_or(row == 4, row == 5), zo, z)

    q_cols = lambda half: pl.ds(pl.multiple_of(half * (8 * HALF), HEAD), 8 * HALF)
    locals_ = [
        pltpu.make_async_copy(k_ref, kin, loc.at[0]),
        pltpu.make_async_copy(v_ref, vin, loc.at[1]),
        pltpu.make_async_copy(q_ref.at[:, q_cols(c)], qbuf.at[c], loc.at[2]),
    ]
    for copy in locals_:
        copy.start()

    barrier = pltpu.get_barrier_semaphore()
    for dev in (dev_xr, dev_xl, dev_z, dev_core, dev_up, dev_down):
        pl.semaphore_signal(barrier, inc=1, device_id=dev, device_id_type=MESH)

    @pl.when(at_end)
    def _():
        pl.semaphore_signal(barrier, inc=1, device_id=dev_outer, device_id_type=MESH)

    pl.semaphore_wait(barrier, jnp.where(at_end, 7, 6))

    def core_copy(src, dst, n):
        return pltpu.make_async_remote_copy(
            src_ref=src, dst_ref=dst, send_sem=core_send.at[n], recv_sem=core_recv.at[n],
            device_id=dev_core, device_id_type=MESH)

    cores = [
        core_copy(q_ref.at[:, q_cols(other)], qbuf.at[c], 0),
        core_copy(stage_s, kv.at[c, z, x], 1),
    ]
    cores[0].start()

    sends = []

    def send(src, dst, dev, cond=None, inside=None):
        place = len(sends)

        def copy():
            return pltpu.make_async_remote_copy(
                src_ref=kv.at[src], dst_ref=kv.at[dst], send_sem=ss.at[place],
                recv_sem=rs.at[dst], device_id=dev, device_id_type=MESH)

        sends.append((copy, [one for one in (cond, inside) if one is not None]))
        if cond is None:
            copy().start()
        else:
            pl.when(cond)(lambda: copy().start())

    def arrived(slot):
        pltpu.make_async_remote_copy(
            src_ref=kv.at[slot], dst_ref=kv.at[slot], send_sem=ss.at[0],
            recv_sem=rs.at[slot], device_id=dev_xr, device_id_type=MESH).wait_recv()

    first_row, not_first, not_last = row == 0, row != 0, row != 7

    def up(src, kind, inside=None):
        send(src, (kind,) + src[1:], dev_up, not_last, inside)

    def own(t):
        for half in range(2):
            slot = (t, z, x, half)
            for dev in (dev_xr, dev_xl, dev_z):
                send(slot, slot, dev)
            up(slot, t + 2)

    def fill(dst, half):
        for g in range(GROUPS):
            cols = pl.ds(pl.multiple_of((half * GROUPS + g) * HEAD, HEAD), HEAD)
            dst[g // 2, 0, g % 2] = kin[:, cols].astype(jnp.float32).T.astype(jnp.bfloat16)
            dst[g // 2, 1, g % 2] = vin[:, cols]

    for copy in locals_[:2]:
        copy.wait()
    fill(stage_s, other)
    cores[1].start()
    fill(kv.at[c, z, x], c)
    own(c)
    cores[1].wait_recv()
    own(other)

    tt = lax.broadcasted_iota(jnp.int32, (TOK, TOK), 0)
    kk = lax.broadcasted_iota(jnp.int32, (TOK, TOK), 1)
    bias_s[...] = jnp.where(kk <= tt, 0.0, -FAR)

    def start_of(i):
        total, first = len_ref[0] * 0, len_ref[0] * 0
        for r in range(8):
            total = total + len_ref[r]
            first = jnp.where(total <= i, total, first)
        return first

    start0, start1 = start_of(2 * row), start_of(2 * row + 1)

    def fine(start, key_inst):
        return jnp.where(start <= key_inst, 0.0, FAR).astype(jnp.float32)

    z1o, z2o = 1 - z1, 1 - z2
    places = {"x": x, "xl": xl, "xr": xr, "xx": xx}

    def slot_of(t, near, place):
        home, away = (z, zo) if t < 2 else (z1, z1o) if t < 4 else (z2, z2o)
        return (t, home if near else away, places[place])

    def event(t, near, place, half):
        slot = slot_of(t, near, place) + (half,)
        inside = None if t < 2 else not_first
        on = lambda *devs: [send(slot, slot, dev, None, inside) for dev in devs]
        arrived(slot)
        if not near:
            if place == "x":
                on(dev_xr, dev_xl)
        elif t < 2:
            if place == "xx":
                on(dev_z)
            elif (t, place) == (0, "xl"):
                on(dev_xr)
            elif (t, place) == (1, "xr"):
                on(dev_xl)
            up(slot, t + 2)
        elif t < 4:
            if place in ("x", "xx"):
                on(dev_z)
            if (t, place) == (3, "x"):
                up(slot, 4, not_first)
        elif place == "x":
            on(dev_xr, dev_xl, dev_z)
        elif place == "xl":
            on(dev_xr)
        elif place == "xx":
            on(dev_z)

    def relay(piece):
        for at, t, place, half in RELAY:
            if at != piece:
                continue
            slot = (t, z, places[place], half)
            arrived(slot)
            send(slot, slot, dev_outer, None, first_row)
            if (t, place) == (3, "x"):
                up(slot, 4, first_row)

    def events_at(piece):
        if any(one[0] == piece for one in RELAY):
            pl.when(first_row)(lambda: relay(piece))
        here = [one[1:] for one in EVENTS if one[0] == piece]
        for common, run_ in itertools.groupby(here, key=lambda one: one[0] < 2):
            several = list(run_)

            def go():
                for one in several:
                    event(*one)

            if common:
                go()
            else:
                pl.when(not_first)(go)

    own_even = fine(start1, 2 * row)
    flags = {(qp, t): fine((start0, start1)[qp], 2 * row + back)
             for qp in range(2) for t, back in ((2, -2), (3, -1), (4, -3))}
    earlier = {
        (near, place): jnp.where(places[place] * 2 + (z if near else zo) < b, 0.0, -FAR).astype(jnp.float32)
        for near in (True, False) for place in places}

    def tiles_of(job, qp):
        tiles = []
        for t, near, place in job:
            slot = slot_of(t, near, place)
            if t == 0 and qp == 1:
                tiles.append((slot, own_even, None))
            elif t == qp:
                tiles.append((slot, None, "own" if near and place == "x" else earlier[near, place]))
            elif t in (2, 3) or (t == 4 and qp == 0):
                tiles.append((slot, flags[qp, t], None))
        return tiles

    def run(number, job, everywhere=False, final=False):
        first = number == 0
        units = [(hb, qp, tiles_of(job, qp)) for qp in range(2) for hb in range(8 // HB)]
        units = [unit for unit in units if unit[2]]

        def compute(g):
            def head_cols(hb, h):
                return pl.ds(pl.multiple_of((g * 8 + hb * HB + h) * HEAD, HEAD), HEAD)

            def scores(unit):
                hb, qp, tiles = unit
                q = jnp.concatenate([qbuf[qp, :, head_cols(hb, h)] for h in range(HB)], axis=0)
                k = jnp.concatenate([kv[slot + (lax.div(g, 2), 0, lax.rem(g, 2))] for slot, _, _ in tiles], axis=1)
                got = jnp.dot(q, k, preferred_element_type=jnp.float32)
                out = []
                for n, (_, _, add) in enumerate(tiles):
                    sc = got[:, n * HEAD:(n + 1) * HEAD]
                    if isinstance(add, str):
                        sc = (sc.reshape(HB, TOK, TOK) + bias_s[...][None]).reshape(ROWS, TOK)
                    elif add is not None:
                        sc = sc + add
                    out.append(sc)
                return out

            def fold(unit, scs):
                hb, qp, tiles = unit
                span = pl.ds(hb * ROWS, ROWS)
                state = g * 2 + qp
                groups = {}
                for sc, (_, pen, _) in zip(scs, tiles):
                    groups.setdefault(id(pen), (pen, []))[1].append(sc)
                best = None
                for pen, members in groups.values():
                    top = members[0]
                    for one in members[1:]:
                        top = jnp.maximum(top, one)
                    top = jnp.max(top, axis=-1, keepdims=True) * SCALE
                    top = top if pen is None else top - pen
                    best = top if best is None else jnp.maximum(best, top)
                best = jnp.broadcast_to(best, (ROWS, HEAD))
                if not first:
                    old = m_s[state, span, :]
                    best = jnp.maximum(old, best)
                    factor = jnp.exp2(old - best)
                shifts = {key: best if pen is None else best + pen for key, (pen, _) in groups.items()}
                ws = [jnp.exp2(sc * SCALE - shifts[id(pen)]) for sc, (_, pen, _) in zip(scs, tiles)]
                total = ws[0]
                for one in ws[1:]:
                    total = total + one
                w = jnp.concatenate([one.astype(jnp.bfloat16) for one in ws], axis=1)
                v = jnp.concatenate([kv[slot + (lax.div(g, 2), 1, lax.rem(g, 2))] for slot, _, _ in tiles], axis=0)
                part = jnp.dot(w, v, preferred_element_type=jnp.float32)
                if not first:
                    total = l_s[state, span, :] * factor + total
                    part = acc_s[state, span, :] * factor + part
                if final:
                    res = (part / jnp.sum(total, axis=-1, keepdims=True)).astype(jnp.bfloat16)
                    for h in range(HB):
                        obuf[qp, :, head_cols(hb, h)] = res[h * TOK:(h + 1) * TOK]
                else:
                    m_s[state, span, :] = best
                    l_s[state, span, :] = total
                    acc_s[state, span, :] = part

            ahead = scores(units[0])
            for n, unit in enumerate(units):
                scs = ahead
                if n + 1 < len(units):
                    ahead = scores(units[n + 1])
                fold(unit, scs)
            if final:
                for copy in results(g):
                    copy.start()

        def body(g, carry):
            for at in range(1, GROUPS):
                if any(e[0] == number * GROUPS + at for e in EVENTS + RELAY):
                    pl.when(g == at)(lambda at=at: events_at(number * GROUPS + at))
            if everywhere:
                compute(g)
            else:
                pl.when(not_first)(lambda: compute(g))
            return carry

        events_at(number * GROUPS)
        lax.fori_loop(0, GROUPS, body, 0)

    def results(g):
        cols = pl.ds(pl.multiple_of(g * (8 * HEAD), HEAD), 8 * HEAD)
        ocols = pl.ds(pl.multiple_of((c * GROUPS + g) * (8 * HEAD), HEAD), 8 * HEAD)
        return (
            pltpu.make_async_copy(obuf.at[c, :, cols], o_ref.at[:, ocols], osem.at[0, g]),
            pltpu.make_async_remote_copy(
                src_ref=obuf.at[other, :, cols], dst_ref=o_ref.at[:, ocols],
                send_sem=osem.at[1, g], recv_sem=osem.at[2, g],
                device_id=dev_core, device_id_type=MESH),
        )

    locals_[2].wait()
    cores[0].wait_recv()
    shared = [job[0][0] < 2 for job in JOBS]
    last_shared = max(n for n, one in enumerate(shared) if one)
    for number in range(last_shared + 1):
        run(number, JOBS[number], everywhere=shared[number])

    @pl.when(first_row)
    def _():
        def body(g, carry):
            for qp in range(2):
                for h in range(8):
                    span = pl.ds(h * TOK, TOK)
                    total = jnp.sum(l_s[g * 2 + qp, span, :], axis=-1, keepdims=True)
                    cols = pl.ds(pl.multiple_of((g * 8 + h) * HEAD, HEAD), HEAD)
                    obuf[qp, :, cols] = (acc_s[g * 2 + qp, span, :] / total).astype(jnp.bfloat16)
            for copy in results(g):
                copy.start()
            return carry

        lax.fori_loop(0, GROUPS, body, 0)

    for number in range(last_shared + 1, len(JOBS)):
        run(number, JOBS[number], final=number == len(JOBS) - 1)

    assert len(sends) <= 112
    for copy, conds in sends:
        if conds:
            cond = conds[0] if len(conds) == 1 else jnp.logical_and(*conds)
            pl.when(cond)(lambda copy=copy: copy().wait_send())
        else:
            copy().wait_send()
    for copy in cores:
        copy.wait_send()
    for g in range(GROUPS):
        mine, theirs = results(g)
        mine.wait()
        theirs.wait()


def local(queries, keys, values, lengths):
    dma = pltpu.SemaphoreType.DMA
    anywhere = pl.BlockSpec(memory_space=pl.ANY)
    return pl.pallas_call(
        kernel,
        out_shape=jax.ShapeDtypeStruct(queries.shape, jnp.bfloat16),
        in_specs=[pl.BlockSpec(memory_space=pltpu.SMEM), anywhere, anywhere, anywhere],
        out_specs=anywhere,
        scratch_shapes=[
            pltpu.VMEM((5, 2, 4, 2, 2, 2, TOK, HEAD), jnp.bfloat16),
            pltpu.VMEM((2, 2, 2, TOK, HEAD), jnp.bfloat16),
            pltpu.VMEM((TOK, 2 * HALF), jnp.bfloat16),
            pltpu.VMEM((TOK, 2 * HALF), jnp.bfloat16),
            pltpu.VMEM((2, TOK, 8 * HALF), jnp.bfloat16),
            pltpu.VMEM((2, TOK, 8 * HALF), jnp.bfloat16),
            pltpu.VMEM((2 * GROUPS, 8 * TOK, HEAD), jnp.float32),
            pltpu.VMEM((2 * GROUPS, 8 * TOK, HEAD), jnp.float32),
            pltpu.VMEM((2 * GROUPS, 8 * TOK, HEAD), jnp.float32),
            pltpu.VMEM((TOK, TOK), jnp.float32),
            dma((5, 2, 4, 2)),
            dma((112,)),
            dma((3,)),
            dma((2,)),
            dma((2,)),
            dma((3, GROUPS)),
        ],
        compiler_params=pltpu.CompilerParams(
            collective_id=0, has_side_effects=True, vmem_limit_bytes=58 * 1024 * 1024),
        cost_estimate=pl.CostEstimate(flops=30_000_000_000, bytes_accessed=8_000_000, transcendentals=40_000_000),
    )(lengths, queries, keys, values)


def solution(mesh):
    split = P(("inst", "blk"), None)
    return jax.shard_map(local, mesh=mesh, in_specs=(split, split, split, P()), out_specs=split, check_vma=False)
```

time: 462 us -> 90.1 us (0.20)
  matrix products: 175 us -> 0 us
  waiting for transfers between devices: 127 us -> 0 us
  Pallas kernels: 0 us -> 86.7 us
  local copies, waits for them, and re-layouts: 77.6 us -> 3.1 us
  other arithmetic: 55.3 us -> 0 us
  between operations: 14.2 us -> 0.01 us
  starting transfers between devices: 10.4 us -> 0 us
    dot_general x32 -> x0, matrix products: 175 us -> none  [the longest x16 141 us: step(): jnp.einsum('chgk,khd->chgd', weights.astype(jnp.bfloat16), value_block, p...]
    pallas_call x0 -> x1, Pallas kernels: none -> 86.7 us  [local(): pl.pallas_call(kernel, out_shape=jax.ShapeDtypeStruct(queries.shape, jnp....]
    all_gather x1 -> x0, waiting for transfers between devices: 81.7 us -> none  [local(): whole = lax.all_gather(stacked, 'blk', axis=1, tiled=True)]
    ppermute x3 -> x0, waiting for transfers between devices: 44.9 us -> none  [passed_along(): return lax.ppermute(value, axis, pairs)]
    reduce_sum x16 -> x0, other arithmetic: 42.9 us -> none  [step(): grand_total = grand_total * factor + jnp.sum(weights, axis=-1)]
    unnamed x14 -> x1, local copies, waits for them, and re-layouts: 35.6 us -> 3.1 us
    dynamic_slice x32 -> x0, local copies, waits for them, and re-layouts: 25.6 us -> none  [absorb(): return lax.scan(step, state, (key_tiles, value_tiles, pos_blocks))[0]]
    while x40 -> x0, local copies, waits for them, and re-layouts: 13.5 us -> none
  transfers between devices with their start and end apart: 4 -> 0, of which waited for: 3 -> 0; matrix products, arithmetic and copies ran while one was open for 46% -> 0% of each run, Pallas kernels for 0% -> 0%
where the time goes in v1:
time: 90.1 us; the launch traced here: 89.8 us
  Pallas kernels  86.7 us (96%)
  local copies, waits for them, and re-layouts  3.1 us (3%)
    pallas_call x1, Pallas kernels, local(): pl.pallas_call(kernel, out_shape=jax.ShapeDtypeStruct(queries.shape, jnp....  86.7 us
    unnamed x1, local copies, waits for them, and re-layouts  3.1 us

profile of v1, /device:TPU:65, one launch (start us, length us, event | category | flops | bytes accessed | tf_op | source)
XLA Modules:
  0.0 89.8 jit_solution(11264375071504687284)
XLA Ops:
  0.0 86.7 %shard_map.46 = bf16[128,8192]{1,0:T(8,128)(2,1)} custom-call(s32[8]{0:T(128)} %len_ref.1, bf16[128,8192]{1,0:T(8,128)(2,1)} %q_ref.1, bf16[128,1024]{1,0:T(8,128)(2,1)} %k_ref.1, bf16[128,1024]{1,0:T(8,128)(2,1)} %v_ref.1), custom_call_target="tpu_custom_call" | custom-call | flops 30000001024 | bytes 8000000 | tf_op jit(solution)/shard_map/pallas_call | solution.py:466
  86.7 3.1 %copy.6 = bf16[128,8192]{1,0:T(8,128)(2,1)} copy(bf16[128,8192]{1,0:T(8,128)(2,1)} %shard_map.46) | data formatting | bytes 4194304

commit v2 on v1

--- a/solution.py
+++ b/solution.py
@@ -30,107 +30,107 @@
     ((2, True, "xx"), (2, False, "xx"), (3, True, "xx"), (3, False, "xx"),),
 )
 EVENTS = (
-    (1, 0, False, "x", 0),
-    (2, 0, False, "x", 1),
-    (3, 2, True, "x", 0),
-    (4, 1, True, "xl", 0),
-    (4, 0, True, "xr", 0),
-    (4, 1, True, "xr", 0),
-    (4, 1, False, "x", 0),
-    (4, 0, True, "xl", 0),
-    (5, 0, True, "xl", 1),
-    (5, 2, True, "x", 1),
-    (6, 3, True, "x", 0),
-    (6, 1, True, "xl", 1),
-    (6, 1, True, "xr", 1),
-    (6, 0, True, "xr", 1),
-    (6, 1, False, "x", 1),
-    (7, 3, True, "x", 1),
-    (7, 0, False, "xl", 1),
-    (7, 0, False, "xr", 1),
-    (7, 0, False, "xr", 0),
-    (7, 0, False, "xl", 0),
-    (7, 2, False, "x", 0),
-    (8, 2, False, "x", 1),
+    (0, 0, False, "x", 1),
+    (0, 0, False, "x", 0),
+    (1, 2, True, "x", 1),
+    (1, 2, True, "x", 0),
+    (1, 0, True, "xl", 0),
+    (1, 1, False, "x", 0),
+    (2, 3, True, "x", 0),
+    (2, 0, True, "xr", 0),
+    (2, 1, True, "xr", 0),
+    (2, 1, False, "x", 1),
+    (2, 1, True, "xl", 0),
+    (3, 3, True, "x", 1),
+    (3, 0, True, "xl", 1),
+    (3, 1, True, "xr", 1),
+    (3, 0, True, "xr", 1),
+    (3, 1, True, "xl", 1),
+    (4, 0, False, "xl", 0),
+    (4, 4, True, "x", 0),
+    (4, 1, True, "xx", 0),
+    (4, 0, False, "xl", 1),
+    (4, 0, True, "xx", 0),
+    (4, 2, False, "x", 0),
+    (4, 3, False, "x", 0),
+    (5, 2, False, "x", 1),
+    (5, 1, False, "xl", 1),
+    (5, 3, False, "x", 1),
+    (5, 1, False, "xr", 0),
+    (6, 0, False, "xr", 1),
+    (6, 1, True, "xx", 1),
+    (6, 1, False, "xl", 0),
+    (6, 1, False, "xr", 1),
+    (6, 2, True, "xr", 0),
+    (6, 0, True, "xx", 1),
+    (6, 0, False, "xx", 0),
+    (6, 4, True, "xl", 0),
+    (6, 3, True, "xr", 0),
+    (6, 1, False, "xx", 0),
+    (6, 0, False, "xr", 0),
+    (7, 2, False, "xr", 0),
+    (7, 4, True, "x", 1),
+    (7, 4, False, "x", 0),
+    (7, 4, True, "xr", 0),
+    (7, 2, False, "xl", 0),
+    (7, 0, False, "xx", 1),
+    (7, 1, False, "xx", 1),
+    (8, 3, True, "xr", 1),
+    (8, 3, False, "xl", 0),
+    (8, 3, False, "xr", 0),
+    (8, 2, False, "xr", 1),
+    (8, 2, True, "xl", 0),
     (8, 3, True, "xl", 0),
-    (8, 1, False, "xl", 0),
-    (8, 1, True, "xx", 0),
-    (8, 3, False, "x", 0),
-    (9, 2, True, "xr", 0),
-    (10, 1, False, "xr", 0),
-    (10, 3, False, "x", 1),
-    (10, 0, True, "xx", 0),
-    (11, 1, True, "xx", 1),
-    (11, 0, True, "xx", 1),
-    (11, 1, False, "xx", 0),
-    (12, 3, True, "xr", 0),
-    (12, 2, True, "xl", 0),
-    (12, 1, False, "xr", 1),
-    (12, 0, False, "xx", 0),
-    (13, 1, False, "xl", 1),
-    (14, 2, False, "xl", 0),
-    (14, 4, True, "x", 0),
-    (14, 1, False, "xx", 1),
-    (14, 2, True, "xl", 1),
-    (14, 0, False, "xx", 1),
-    (16, 3, True, "xl", 1),
-    (16, 4, False, "x", 0),
-    (18, 2, True, "xr", 1),
-    (18, 2, False, "xr", 0),
-    (18, 3, True, "xr", 1),
-    (19, 4, True, "x", 1),
-    (20, 4, True, "xl", 0),
-    (20, 4, True, "xr", 0),
-    (21, 3, True, "xx", 0),
-    (22, 3, False, "xr", 1),
-    (22, 3, False, "xr", 0),
-    (22, 4, True, "xl", 1),
-    (22, 4, True, "xr", 1),
-    (22, 3, False, "xl", 0),
-    (22, 4, False, "x", 1),
-    (22, 3, False, "xl", 1),
-    (23, 2, False, "xl", 1),
-    (23, 2, True, "xx", 0),
-    (24, 4, False, "xr", 0),
-    (24, 4, True, "xx", 0),
-    (25, 4, False, "xr", 1),
-    (26, 4, True, "xx", 1),
-    (26, 2, False, "xr", 1),
-    (27, 4, False, "xl", 1),
-    (28, 4, False, "xx", 0),
-    (28, 3, True, "xx", 1),
-    (28, 2, True, "xx", 1),
-    (28, 4, False, "xl", 0),
-    (30, 4, False, "xx", 1),
-    (31, 3, False, "xx", 0),
-    (32, 2, False, "xx", 0),
-    (32, 3, False, "xx", 1),
-    (34, 2, False, "xx", 1),
+    (9, 2, True, "xl", 1),
+    (9, 3, False, "xl", 1),
+    (9, 2, False, "xl", 1),
+    (9, 3, False, "xr", 1),
+    (9, 2, True, "xr", 1),
+    (9, 3, True, "xl", 1),
+    (9, 4, True, "xx", 0),
+    (10, 3, True, "xx", 0),
+    (10, 4, True, "xl", 1),
+    (11, 4, True, "xr", 1),
+    (11, 4, False, "x", 1),
+    (12, 2, True, "xx", 0),
+    (13, 4, True, "xx", 1),
+    (13, 4, False, "xx", 0),
+    (14, 2, True, "xx", 1),
+    (14, 4, False, "xl", 0),
+    (14, 4, False, "xr", 0),
+    (15, 4, False, "xl", 1),
+    (15, 3, True, "xx", 1),
+    (15, 4, False, "xx", 1),
+    (15, 4, False, "xr", 1),
+    (16, 3, False, "xx", 0),
+    (16, 2, False, "xx", 0),
+    (17, 2, False, "xx", 1),
+    (17, 3, False, "xx", 1),
 )
 RELAY = (
     (0, 2, "x", 0),
-    (3, 2, "x", 1),
-    (4, 3, "x", 0),
-    (5, 3, "x", 1),
-    (6, 3, "xl", 0),
-    (6, 2, "xr", 0),
-    (7, 3, "xr", 0),
-    (8, 2, "xl", 0),
-    (9, 2, "xl", 1),
-    (10, 4, "x", 0),
-    (12, 3, "xl", 1),
-    (12, 3, "xr", 1),
-    (13, 2, "xr", 1),
-    (14, 4, "x", 1),
-    (14, 3, "xx", 0),
-    (15, 2, "xx", 0),
-    (15, 3, "xx", 1),
-    (15, 2, "xx", 1),
+    (0, 2, "x", 1),
+    (0, 3, "x", 0),
+    (1, 3, "x", 1),
+    (1, 2, "xl", 0),
+    (1, 4, "x", 0),
+    (1, 2, "xr", 0),
+    (2, 3, "xr", 0),
+    (3, 3, "xl", 0),
+    (3, 4, "x", 1),
+    (4, 2, "xl", 1),
+    (5, 3, "xr", 1),
+    (5, 2, "xr", 1),
+    (6, 3, "xl", 1),
+    (6, 3, "xx", 0),
+    (7, 2, "xx", 0),
+    (7, 3, "xx", 1),
+    (7, 2, "xx", 1),
 )
 
 
-def kernel(len_ref, q_ref, k_ref, v_ref, o_ref, kv, stage_s, kin, vin, qbuf, obuf, acc_s, m_s, l_s, bias_s,
-           rs, ss, loc, core_send, core_recv, osem):
+def kernel(len_hbm, q_ref, k_ref, v_ref, o_ref, kv, stage_s, kin, vin, qbuf, qs, obuf, acc_s, m_s, l_s, bias_s,
+           len_ref, rs, ss, loc, core_send, core_recv, osem):
     inst, b = lax.axis_index("inst"), lax.axis_index("blk")
     c, row = lax.rem(inst, 2), inst // 2
     other = 1 - c
@@ -153,6 +153,7 @@
         pltpu.make_async_copy(k_ref, kin, loc.at[0]),
         pltpu.make_async_copy(v_ref, vin, loc.at[1]),
         pltpu.make_async_copy(q_ref.at[:, q_cols(c)], qbuf.at[c], loc.at[2]),
+        pltpu.make_async_copy(len_hbm, len_ref, loc.at[3]),
     ]
     for copy in locals_:
         copy.start()
@@ -229,6 +230,8 @@
     tt = lax.broadcasted_iota(jnp.int32, (TOK, TOK), 0)
     kk = lax.broadcasted_iota(jnp.int32, (TOK, TOK), 1)
     bias_s[...] = jnp.where(kk <= tt, 0.0, -FAR)
+
+    locals_[3].wait()
 
     def start_of(i):
         total, first = len_ref[0] * 0, len_ref[0] * 0
@@ -324,18 +327,22 @@
 
     def run(number, job, everywhere=False, final=False):
         first = number == 0
-        units = [(hb, qp, tiles_of(job, qp)) for qp in range(2) for hb in range(8 // HB)]
-        units = [unit for unit in units if unit[2]]
-
-        def compute(g):
-            def head_cols(hb, h):
+        units = [(gg, hb, qp, tiles_of(job, qp)) for gg in range(2) for qp in range(2) for hb in range(8 // HB)]
+        units = [unit for unit in units if unit[3]]
+
+        def compute(pair):
+            def head_cols(g, hb, h):
                 return pl.ds(pl.multiple_of((g * 8 + hb * HB + h) * HEAD, HEAD), HEAD)
 
+            def wide_cols(g, hb, h):
+                return pl.ds(pl.multiple_of((g * 8 + hb * HB + h) * (2 * HEAD), 2 * HEAD), 2 * HEAD)
+
             def scores(unit):
-                hb, qp, tiles = unit
-                q = jnp.concatenate([qbuf[qp, :, head_cols(hb, h)] for h in range(HB)], axis=0)
-                k = jnp.concatenate([kv[slot + (lax.div(g, 2), 0, lax.rem(g, 2))] for slot, _, _ in tiles], axis=1)
-                got = jnp.dot(q, k, preferred_element_type=jnp.float32)
+                gg, hb, qp, tiles = unit
+                g = pair * 2 + gg
+                q = jnp.concatenate([qs[qp, :, wide_cols(g, hb, h)] for h in range(HB)], axis=0)
+                k = jnp.concatenate([kv[slot + (pair, 0, gg)] for slot, _, _ in tiles], axis=1)
+                got = jnp.dot(q, jnp.concatenate([k, k], axis=0), preferred_element_type=jnp.float32)
                 out = []
                 for n, (_, _, add) in enumerate(tiles):
                     sc = got[:, n * HEAD:(n + 1) * HEAD]
@@ -347,7 +354,8 @@
                 return out
 
             def fold(unit, scs):
-                hb, qp, tiles = unit
+                gg, hb, qp, tiles = unit
+                g = pair * 2 + gg
                 span = pl.ds(hb * ROWS, ROWS)
                 state = g * 2 + qp
                 groups = {}
@@ -358,7 +366,7 @@
                     top = members[0]
                     for one in members[1:]:
                         top = jnp.maximum(top, one)
-                    top = jnp.max(top, axis=-1, keepdims=True) * SCALE
+                    top = jnp.max(top, axis=-1, keepdims=True)
                     top = top if pen is None else top - pen
                     best = top if best is None else jnp.maximum(best, top)
                 best = jnp.broadcast_to(best, (ROWS, HEAD))
@@ -367,20 +375,19 @@
                     best = jnp.maximum(old, best)
                     factor = jnp.exp2(old - best)
                 shifts = {key: best if pen is None else best + pen for key, (pen, _) in groups.items()}
-                ws = [jnp.exp2(sc * SCALE - shifts[id(pen)]) for sc, (_, pen, _) in zip(scs, tiles)]
-                total = ws[0]
-                for one in ws[1:]:
-                    total = total + one
+                ws = [jnp.exp2(sc - shifts[id(pen)]) for sc, (_, pen, _) in zip(scs, tiles)]
                 w = jnp.concatenate([one.astype(jnp.bfloat16) for one in ws], axis=1)
-                v = jnp.concatenate([kv[slot + (lax.div(g, 2), 1, lax.rem(g, 2))] for slot, _, _ in tiles], axis=0)
-                part = jnp.dot(w, v, preferred_element_type=jnp.float32)
+                v = jnp.concatenate([kv[slot + (pair, 1, gg)] for slot, _, _ in tiles], axis=0)
+                v = jnp.concatenate([v, jnp.ones_like(v)], axis=1)
+                both = jnp.dot(w, v, preferred_element_type=jnp.float32)
+                part, total = both[:, :HEAD], both[:, HEAD:]
                 if not first:
                     total = l_s[state, span, :] * factor + total
                     part = acc_s[state, span, :] * factor + part
                 if final:
-                    res = (part / jnp.sum(total, axis=-1, keepdims=True)).astype(jnp.bfloat16)
+                    res = (part / total).astype(jnp.bfloat16)
                     for h in range(HB):
-                        obuf[qp, :, head_cols(hb, h)] = res[h * TOK:(h + 1) * TOK]
+                        obuf[qp, :, head_cols(g, hb, h)] = res[h * TOK:(h + 1) * TOK]
                 else:
                     m_s[state, span, :] = best
                     l_s[state, span, :] = total
@@ -392,22 +399,21 @@
                 if n + 1 < len(units):
                     ahead = scores(units[n + 1])
                 fold(unit, scs)
-            if final:
-                for copy in results(g):
-                    copy.start()
-
-        def body(g, carry):
-            for at in range(1, GROUPS):
-                if any(e[0] == number * GROUPS + at for e in EVENTS + RELAY):
-                    pl.when(g == at)(lambda at=at: events_at(number * GROUPS + at))
+                if final and unit[0] != (units + [(None,)])[n + 1][0]:
+                    for copy in results(pair * 2 + unit[0]):
+                        copy.start()
+
+        def body(pair, carry):
+            if any(e[0] == number * 2 + 1 for e in EVENTS + RELAY):
+                pl.when(pair == 1)(lambda: events_at(number * 2 + 1))
             if everywhere:
-                compute(g)
+                compute(pair)
             else:
-                pl.when(not_first)(lambda: compute(g))
+                pl.when(not_first)(lambda: compute(pair))
             return carry
 
-        events_at(number * GROUPS)
-        lax.fori_loop(0, GROUPS, body, 0)
+        events_at(number * 2)
+        lax.fori_loop(0, 2, body, 0)
 
     def results(g):
         cols = pl.ds(pl.multiple_of(g * (8 * HEAD), HEAD), 8 * HEAD)
@@ -422,6 +428,17 @@
 
     locals_[2].wait()
     cores[0].wait_recv()
+
+    def scale(h, carry):
+        for qp in range(2):
+            q = qbuf[qp, :, pl.ds(pl.multiple_of(h * HEAD, HEAD), HEAD)].astype(jnp.float32) * SCALE
+            high = q.astype(jnp.bfloat16)
+            low = (q - high.astype(jnp.float32)).astype(jnp.bfloat16)
+            qs[qp, :, pl.ds(pl.multiple_of(h * (2 * HEAD), HEAD), HEAD)] = high
+            qs[qp, :, pl.ds(pl.multiple_of(h * (2 * HEAD) + HEAD, HEAD), HEAD)] = low
+        return carry
+
+    lax.fori_loop(0, 8 * GROUPS, scale, 0, unroll=4)
     shared = [job[0][0] < 2 for job in JOBS]
     last_shared = max(n for n, one in enumerate(shared) if one)
     for number in range(last_shared + 1):
@@ -433,7 +450,7 @@
             for qp in range(2):
                 for h in range(8):
                     span = pl.ds(h * TOK, TOK)
-                    total = jnp.sum(l_s[g * 2 + qp, span, :], axis=-1, keepdims=True)
+                    total = l_s[g * 2 + qp, span, :]
                     cols = pl.ds(pl.multiple_of((g * 8 + h) * HEAD, HEAD), HEAD)
                     obuf[qp, :, cols] = (acc_s[g * 2 + qp, span, :] / total).astype(jnp.bfloat16)
             for copy in results(g):
@@ -463,10 +480,12 @@
 def local(queries, keys, values, lengths):
     dma = pltpu.SemaphoreType.DMA
     anywhere = pl.BlockSpec(memory_space=pl.ANY)
+    queries, keys, values, lengths = (
+        pltpu.with_memory_space_constraint(one, pltpu.HBM) for one in (queries, keys, values, lengths))
     return pl.pallas_call(
         kernel,
         out_shape=jax.ShapeDtypeStruct(queries.shape, jnp.bfloat16),
-        in_specs=[pl.BlockSpec(memory_space=pltpu.SMEM), anywhere, anywhere, anywhere],
+        in_specs=[anywhere] * 4,
         out_specs=anywhere,
         scratch_shapes=[
             pltpu.VMEM((5, 2, 4, 2, 2, 2, TOK, HEAD), jnp.bfloat16),
@@ -474,20 +493,22 @@
             pltpu.VMEM((TOK, 2 * HALF), jnp.bfloat16),
             pltpu.VMEM((TOK, 2 * HALF), jnp.bfloat16),
             pltpu.VMEM((2, TOK, 8 * HALF), jnp.bfloat16),
+            pltpu.VMEM((2, TOK, 16 * HALF), jnp.bfloat16),
             pltpu.VMEM((2, TOK, 8 * HALF), jnp.bfloat16),
             pltpu.VMEM((2 * GROUPS, 8 * TOK, HEAD), jnp.float32),
             pltpu.VMEM((2 * GROUPS, 8 * TOK, HEAD), jnp.float32),
             pltpu.VMEM((2 * GROUPS, 8 * TOK, HEAD), jnp.float32),
             pltpu.VMEM((TOK, TOK), jnp.float32),
+            pltpu.SMEM((8,), jnp.int32),
             dma((5, 2, 4, 2)),
             dma((112,)),
-            dma((3,)),
+            dma((4,)),
             dma((2,)),
             dma((2,)),
             dma((3, GROUPS)),
         ],
         compiler_params=pltpu.CompilerParams(
-            collective_id=0, has_side_effects=True, vmem_limit_bytes=58 * 1024 * 1024),
+            collective_id=0, has_side_effects=True, vmem_limit_bytes=44 * 1024 * 1024),
         cost_estimate=pl.CostEstimate(flops=30_000_000_000, bytes_accessed=8_000_000, transcendentals=40_000_000),
     )(lengths, queries, keys, values)
 

time: 90.1 us -> 82.2 us (0.912)
  Pallas kernels: 86.7 us -> 80.8 us
  local copies, waits for them, and re-layouts: 3.1 us -> 1.32 us
    pallas_call x1, Pallas kernels: 86.7 us -> 80.8 us  [local(): pl.pallas_call(kernel, out_shape=jax.ShapeDtypeStruct(queries.shape, jnp....]
    unnamed x1, local copies, waits for them, and re-layouts: 3.1 us -> 1.32 us
where the time goes in v2:
time: 82.2 us; the launch traced here: 82.1 us
  Pallas kernels  80.8 us (98%)
  local copies, waits for them, and re-layouts  1.32 us (2%)
    pallas_call x1, Pallas kernels, local(): pl.pallas_call(kernel, out_shape=jax.ShapeDtypeStruct(queries.shape, jnp....  80.8 us

profile of v2, /device:TPU:65, one launch (start us, length us, event | category | flops | bytes accessed | tf_op | source)
XLA Modules:
  0.0 82.1 jit_solution(9898762649553787737)
XLA Ops:
  0.0 80.8 %shard_map.46 = bf16[128,8192]{1,0:T(8,128)(2,1)S(1)} custom-call(s32[8]{0:T(128)} %len_hbm.1, bf16[128,8192]{1,0:T(8,128)(2,1)} %q_ref.1, bf16[128,1024]{1,0:T(8,128)(2,1)} %k_ref.1, bf16[128,1024]{1,0:T(8,128)(2,1)} %v_ref.1), custom_call_target="tpu_custom_call" | custom-call | flops 30000001024 | bytes 8000000 | tf_op jit(solution)/shard_map/pallas_call | solution.py:485
  80.8 1.3 %copy.6 = bf16[128,8192]{1,0:T(8,128)(2,1)} copy(bf16[128,8192]{1,0:T(8,128)(2,1)S(1)} %shard_map.46) | data formatting | bytes 4194304

commit v3 on v2

--- a/solution.py
+++ b/solution.py
@@ -20,112 +20,113 @@
 
 JOBS = (
     ((0, True, "x"), (1, True, "x"),),
-    ((0, True, "xl"), (1, True, "xl"), (0, True, "xr"), (1, True, "xr"), (0, False, "x"), (1, False, "x"),),
+    ((0, True, "xl"), (0, True, "xr"), (0, False, "x"),),
+    ((1, True, "xl"), (1, True, "xr"), (1, False, "x"),),
     ((2, True, "x"), (3, True, "x"), (2, False, "x"), (3, False, "x"),),
-    ((0, False, "xl"), (0, False, "xr"), (0, True, "xx"), (0, False, "xx"), (1, False, "xl"), (1, False, "xr"), (1, True, "xx"), (1, False, "xx"),),
-    ((2, True, "xl"), (2, True, "xr"), (3, True, "xl"), (3, True, "xr"),),
-    ((4, True, "x"), (4, False, "x"), (4, True, "xl"), (4, True, "xr"),),
-    ((2, False, "xl"), (2, False, "xr"), (3, False, "xl"), (3, False, "xr"),),
-    ((4, True, "xx"), (4, False, "xx"), (4, False, "xl"), (4, False, "xr"),),
-    ((2, True, "xx"), (2, False, "xx"), (3, True, "xx"), (3, False, "xx"),),
+    ((0, False, "xl"), (0, False, "xr"), (0, True, "xx"), (1, False, "xl"), (1, False, "xr"), (1, True, "xx"),),
+    ((0, False, "xx"), (1, False, "xx"),),
+    ((2, True, "xl"), (2, True, "xr"), (3, True, "xl"), (3, True, "xr"), (4, True, "x"), (4, False, "x"),),
+    ((2, False, "xl"), (2, False, "xr"), (3, False, "xl"), (3, False, "xr"), (4, True, "xl"), (4, True, "xr"),),
+    ((2, True, "xx"), (3, True, "xx"), (4, True, "xx"), (4, False, "xl"), (4, False, "xr"),),
+    ((2, False, "xx"), (3, False, "xx"), (4, False, "xx"),),
 )
 EVENTS = (
+    (0, 2, True, "x", 0),
     (0, 0, False, "x", 1),
+    (0, 2, True, "x", 1),
     (0, 0, False, "x", 0),
-    (1, 2, True, "x", 1),
-    (1, 2, True, "x", 0),
+    (1, 3, True, "x", 0),
+    (1, 0, True, "xl", 1),
+    (1, 1, True, "xr", 0),
     (1, 0, True, "xl", 0),
-    (1, 1, False, "x", 0),
-    (2, 3, True, "x", 0),
+    (1, 1, False, "x", 1),
+    (1, 1, True, "xr", 1),
+    (2, 3, True, "x", 1),
     (2, 0, True, "xr", 0),
-    (2, 1, True, "xr", 0),
-    (2, 1, False, "x", 1),
-    (2, 1, True, "xl", 0),
-    (3, 3, True, "x", 1),
-    (3, 0, True, "xl", 1),
-    (3, 1, True, "xr", 1),
-    (3, 0, True, "xr", 1),
+    (2, 0, True, "xr", 1),
+    (3, 1, True, "xl", 0),
     (3, 1, True, "xl", 1),
-    (4, 0, False, "xl", 0),
+    (3, 0, False, "xl", 1),
     (4, 4, True, "x", 0),
-    (4, 1, True, "xx", 0),
-    (4, 0, False, "xl", 1),
-    (4, 0, True, "xx", 0),
-    (4, 2, False, "x", 0),
+    (4, 0, True, "xx", 1),
+    (4, 0, False, "xr", 0),
+    (4, 1, False, "x", 0),
     (4, 3, False, "x", 0),
-    (5, 2, False, "x", 1),
-    (5, 1, False, "xl", 1),
-    (5, 3, False, "x", 1),
-    (5, 1, False, "xr", 0),
-    (6, 0, False, "xr", 1),
-    (6, 1, True, "xx", 1),
-    (6, 1, False, "xl", 0),
-    (6, 1, False, "xr", 1),
-    (6, 2, True, "xr", 0),
-    (6, 0, True, "xx", 1),
-    (6, 0, False, "xx", 0),
-    (6, 4, True, "xl", 0),
+    (5, 0, True, "xx", 0),
     (6, 3, True, "xr", 0),
-    (6, 1, False, "xx", 0),
-    (6, 0, False, "xr", 0),
-    (7, 2, False, "xr", 0),
-    (7, 4, True, "x", 1),
-    (7, 4, False, "x", 0),
-    (7, 4, True, "xr", 0),
-    (7, 2, False, "xl", 0),
-    (7, 0, False, "xx", 1),
-    (7, 1, False, "xx", 1),
-    (8, 3, True, "xr", 1),
-    (8, 3, False, "xl", 0),
-    (8, 3, False, "xr", 0),
-    (8, 2, False, "xr", 1),
-    (8, 2, True, "xl", 0),
-    (8, 3, True, "xl", 0),
-    (9, 2, True, "xl", 1),
-    (9, 3, False, "xl", 1),
-    (9, 2, False, "xl", 1),
-    (9, 3, False, "xr", 1),
-    (9, 2, True, "xr", 1),
-    (9, 3, True, "xl", 1),
-    (9, 4, True, "xx", 0),
-    (10, 3, True, "xx", 0),
-    (10, 4, True, "xl", 1),
-    (11, 4, True, "xr", 1),
-    (11, 4, False, "x", 1),
-    (12, 2, True, "xx", 0),
-    (13, 4, True, "xx", 1),
-    (13, 4, False, "xx", 0),
+    (6, 2, False, "x", 0),
+    (7, 2, False, "x", 1),
+    (7, 1, True, "xx", 0),
+    (7, 1, False, "xl", 1),
+    (7, 0, False, "xr", 1),
+    (7, 2, True, "xl", 0),
+    (7, 1, True, "xx", 1),
+    (7, 2, True, "xl", 1),
+    (7, 0, False, "xl", 0),
+    (7, 1, False, "xr", 1),
+    (7, 4, True, "xl", 0),
+    (7, 3, False, "x", 1),
+    (8, 0, False, "xx", 0),
+    (8, 1, False, "xr", 0),
+    (8, 1, False, "xl", 0),
+    (10, 0, False, "xx", 1),
+    (10, 4, True, "x", 1),
+    (10, 1, False, "xx", 0),
+    (10, 4, False, "x", 0),
+    (10, 2, True, "xr", 0),
+    (11, 3, True, "xr", 1),
+    (11, 1, False, "xx", 1),
+    (12, 3, True, "xl", 0),
+    (12, 2, False, "xl", 1),
+    (12, 3, False, "xr", 0),
+    (13, 4, True, "xx", 0),
+    (13, 3, True, "xl", 1),
+    (13, 2, True, "xr", 1),
+    (13, 4, False, "x", 1),
     (14, 2, True, "xx", 1),
-    (14, 4, False, "xl", 0),
+    (14, 2, False, "xr", 0),
+    (14, 4, True, "xr", 1),
+    (14, 4, True, "xr", 0),
+    (14, 4, False, "xx", 0),
+    (14, 3, False, "xr", 1),
+    (14, 2, False, "xl", 0),
+    (14, 3, False, "xl", 1),
     (14, 4, False, "xr", 0),
-    (15, 4, False, "xl", 1),
-    (15, 3, True, "xx", 1),
-    (15, 4, False, "xx", 1),
+    (14, 2, False, "xr", 1),
+    (14, 4, True, "xl", 1),
+    (14, 3, False, "xl", 0),
+    (14, 2, True, "xx", 0),
+    (15, 3, True, "xx", 0),
+    (15, 2, False, "xx", 1),
     (15, 4, False, "xr", 1),
-    (16, 3, False, "xx", 0),
+    (16, 4, False, "xl", 1),
+    (16, 3, True, "xx", 1),
     (16, 2, False, "xx", 0),
-    (17, 2, False, "xx", 1),
-    (17, 3, False, "xx", 1),
+    (16, 4, False, "xl", 0),
+    (17, 3, False, "xx", 0),
+    (17, 4, True, "xx", 1),
+    (19, 3, False, "xx", 1),
+    (19, 4, False, "xx", 1),
 )
 RELAY = (
     (0, 2, "x", 0),
     (0, 2, "x", 1),
     (0, 3, "x", 0),
     (1, 3, "x", 1),
-    (1, 2, "xl", 0),
     (1, 4, "x", 0),
-    (1, 2, "xr", 0),
+    (2, 2, "xl", 1),
     (2, 3, "xr", 0),
-    (3, 3, "xl", 0),
+    (2, 2, "xl", 0),
+    (3, 3, "xr", 1),
     (3, 4, "x", 1),
-    (4, 2, "xl", 1),
-    (5, 3, "xr", 1),
-    (5, 2, "xr", 1),
-    (6, 3, "xl", 1),
-    (6, 3, "xx", 0),
-    (7, 2, "xx", 0),
-    (7, 3, "xx", 1),
+    (4, 2, "xr", 0),
+    (4, 2, "xr", 1),
+    (5, 3, "xl", 0),
+    (7, 3, "xl", 1),
     (7, 2, "xx", 1),
+    (8, 2, "xx", 0),
+    (9, 3, "xx", 0),
+    (10, 3, "xx", 1),
 )
 
 
@@ -179,7 +180,17 @@
     ]
     cores[0].start()
 
-    sends = []
+    sends, drained, job_now = [], [0], [0]
+
+    def drain(before):
+        while drained[0] < len(sends) and sends[drained[0]][2] < before:
+            copy, conds, _ = sends[drained[0]]
+            drained[0] += 1
+            if conds:
+                cond = conds[0] if len(conds) == 1 else jnp.logical_and(*conds)
+                pl.when(cond)(lambda: copy().wait_send())
+            else:
+                copy().wait_send()
 
     def send(src, dst, dev, cond=None, inside=None):
         place = len(sends)
@@ -189,7 +200,7 @@
                 src_ref=kv.at[src], dst_ref=kv.at[dst], send_sem=ss.at[place],
                 recv_sem=rs.at[dst], device_id=dev, device_id_type=MESH)
 
-        sends.append((copy, [one for one in (cond, inside) if one is not None]))
+        sends.append((copy, [one for one in (cond, inside) if one is not None], job_now[0]))
         if cond is None:
             copy().start()
         else:
@@ -220,10 +231,10 @@
 
     for copy in locals_[:2]:
         copy.wait()
+    fill(kv.at[c, z, x], c)
+    own(c)
     fill(stage_s, other)
     cores[1].start()
-    fill(kv.at[c, z, x], c)
-    own(c)
     cores[1].wait_recv()
     own(other)
 
@@ -412,6 +423,8 @@
                 pl.when(not_first)(lambda: compute(pair))
             return carry
 
+        job_now[0] = number
+        drain(number - 2)
         events_at(number * 2)
         lax.fori_loop(0, 2, body, 0)
 
@@ -463,12 +476,7 @@
         run(number, JOBS[number], final=number == len(JOBS) - 1)
 
     assert len(sends) <= 112
-    for copy, conds in sends:
-        if conds:
-            cond = conds[0] if len(conds) == 1 else jnp.logical_and(*conds)
-            pl.when(cond)(lambda copy=copy: copy().wait_send())
-        else:
-            copy().wait_send()
+    drain(len(JOBS))
     for copy in cores:
         copy.wait_send()
     for g in range(GROUPS):

time: 82.2 us -> 92.7 us (1.13)
  Pallas kernels: 80.8 us -> 91.2 us
    pallas_call x1, Pallas kernels: 80.8 us -> 91.2 us  [local(): pl.pallas_call(kernel, out_shape=jax.ShapeDtypeStruct(queries.shape, jnp....]
where the time goes in v3:
time: 92.7 us; the launch traced here: 92.5 us
  Pallas kernels  91.2 us (98%)
  local copies, waits for them, and re-layouts  1.32 us (1%)
    pallas_call x1, Pallas kernels, local(): pl.pallas_call(kernel, out_shape=jax.ShapeDtypeStruct(queries.shape, jnp....  91.2 us

profile of v3, /device:TPU:65, one launch (start us, length us, event | category | flops | bytes accessed | tf_op | source)
XLA Modules:
  0.0 92.5 jit_solution(17951629474106348147)
XLA Ops:
  0.0 91.2 %shard_map.46 = bf16[128,8192]{1,0:T(8,128)(2,1)S(1)} custom-call(s32[8]{0:T(128)} %len_hbm.1, bf16[128,8192]{1,0:T(8,128)(2,1)} %q_ref.1, bf16[128,1024]{1,0:T(8,128)(2,1)} %k_ref.1, bf16[128,1024]{1,0:T(8,128)(2,1)} %v_ref.1), custom_call_target="tpu_custom_call" | custom-call | flops 30000001024 | bytes 8000000 | tf_op jit(solution)/shard_map/pallas_call | solution.py:493
  91.2 1.3 %copy.6 = bf16[128,8192]{1,0:T(8,128)(2,1)} copy(bf16[128,8192]{1,0:T(8,128)(2,1)S(1)} %shard_map.46) | data formatting | bytes 4194304

commit v4 on v2

--- a/solution.py
+++ b/solution.py
@@ -179,7 +179,17 @@
     ]
     cores[0].start()
 
-    sends = []
+    sends, drained, job_now = [], [0], [0]
+
+    def drain(before):
+        while drained[0] < len(sends) and sends[drained[0]][2] < before:
+            copy, conds, _ = sends[drained[0]]
+            drained[0] += 1
+            if conds:
+                cond = conds[0] if len(conds) == 1 else jnp.logical_and(*conds)
+                pl.when(cond)(lambda: copy().wait_send())
+            else:
+                copy().wait_send()
 
     def send(src, dst, dev, cond=None, inside=None):
         place = len(sends)
@@ -189,7 +199,7 @@
                 src_ref=kv.at[src], dst_ref=kv.at[dst], send_sem=ss.at[place],
                 recv_sem=rs.at[dst], device_id=dev, device_id_type=MESH)
 
-        sends.append((copy, [one for one in (cond, inside) if one is not None]))
+        sends.append((copy, [one for one in (cond, inside) if one is not None], job_now[0]))
         if cond is None:
             copy().start()
         else:
@@ -220,10 +230,10 @@
 
     for copy in locals_[:2]:
         copy.wait()
+    fill(kv.at[c, z, x], c)
+    own(c)
     fill(stage_s, other)
     cores[1].start()
-    fill(kv.at[c, z, x], c)
-    own(c)
     cores[1].wait_recv()
     own(other)
 
@@ -412,6 +422,9 @@
                 pl.when(not_first)(lambda: compute(pair))
             return carry
 
+        job_now[0] = number
+        if number == len(JOBS) - 1:
+            drain(number - 2)
         events_at(number * 2)
         lax.fori_loop(0, 2, body, 0)
 
@@ -463,12 +476,7 @@
         run(number, JOBS[number], final=number == len(JOBS) - 1)
 
     assert len(sends) <= 112
-    for copy, conds in sends:
-        if conds:
-            cond = conds[0] if len(conds) == 1 else jnp.logical_and(*conds)
-            pl.when(cond)(lambda copy=copy: copy().wait_send())
-        else:
-            copy().wait_send()
+    drain(len(JOBS))
     for copy in cores:
         copy.wait_send()
     for g in range(GROUPS):

time: 82.2 us -> 82.2 us (level)
  no operation moved by 1% of the time
where the time goes in v4:
time: 82.2 us; the launch traced here: 82.1 us
  Pallas kernels  80.8 us (98%)
  local copies, waits for them, and re-layouts  1.32 us (2%)
    pallas_call x1, Pallas kernels, local(): pl.pallas_call(kernel, out_shape=jax.ShapeDtypeStruct(queries.shape, jnp....  80.8 us

profile of v4, /device:TPU:65, one launch (start us, length us, event | category | flops | bytes accessed | tf_op | source)
XLA Modules:
  0.0 82.1 jit_solution(375988501724030387)
XLA Ops:
  0.0 80.8 %shard_map.46 = bf16[128,8192]{1,0:T(8,128)(2,1)S(1)} custom-call(s32[8]{0:T(128)} %len_hbm.1, bf16[128,8192]{1,0:T(8,128)(2,1)} %q_ref.1, bf16[128,1024]{1,0:T(8,128)(2,1)} %k_ref.1, bf16[128,1024]{1,0:T(8,128)(2,1)} %v_ref.1), custom_call_target="tpu_custom_call" | custom-call | flops 30000001024 | bytes 8000000 | tf_op jit(solution)/shard_map/pallas_call | solution.py:493
  80.8 1.3 %copy.6 = bf16[128,8192]{1,0:T(8,128)(2,1)} copy(bf16[128,8192]{1,0:T(8,128)(2,1)S(1)} %shard_map.46) | data formatting | bytes 4194304
